TPU v7x, 32 devices: a whole 2x2x4 slice. The times are simulated.
32 devices in a mesh: replica: 4 (over y, core), fsdp: 8 (over z, x).
Axes of the slice: x: 2, y: 2, z: 4, core: 2. Of those that a mesh axis runs over, the one named last changes fastest.
Arguments:
- anchor_params: bfloat16 [24, 512, 4096], P(None, 'fsdp')
- replica_params: bfloat16 [4, 24, 512, 4096], P('replica', None, 'fsdp')
- projection: bfloat16 [4096, 384], replicated
- momentum: float32 [24, 512, 384], P(None, 'fsdp'), may hold values from -1.8 to 1.8
- rate_table: float32 [4, 6], replicated, may hold values from 0.1 to 1
- owner_list: int32 [24], replicated, may hold values from 0 to 7, as said below
- layer_kind: int32 [24, 2], replicated, may hold values from 0 to 5, as said below
Outputs:
- new_params: bfloat16 [24, 512, 4096], P(None, 'fsdp')
- new_momentum: float32 [24, 512, 384], P(None, 'fsdp')
Inputs may be any that keep to these rules, and one draw needn't show every extreme that they name: `owner_list`: no fsdp index is named more than 4 times, and in every draw some index is named exactly 4 times. `layer_kind`: column 0 is a layer, column 1 a kind below 6; each layer has 6 rows, and no two rows are equal.
All inputs are finite; a program needn't handle non-finite values.
Results may differ from a plain program's by a relative error of at most 0.0055.
Values may be sent and summed in bfloat16 or wider, within the bound.
A program may use at most 128 MiB of HBM per device.

v0:
```python
import jax
import jax.numpy as jnp
from jax import lax
from jax.sharding import PartitionSpec as P

OUTER_MOMENTUM = 0.9
EPSILON = 1e-06


def local(anchor_params, replica_params, projection, momentum, rate_table, owner_list, layer_kind):
    matrices, rows_dev, model_width = anchor_params.shape
    rank_dim = projection.shape[1]
    all_rows = rows_dev * lax.axis_size("fsdp")
    pseudo_grad = (
        anchor_params.astype(jnp.float32) - replica_params[0].astype(jnp.float32)
    ).astype(jnp.bfloat16)
    compressed = jnp.dot(
        pseudo_grad.reshape(matrices * rows_dev, model_width),
        projection,
        preferred_element_type=jnp.float32,
    )
    summed = lax.psum(compressed.reshape(matrices, rows_dev, rank_dim), "replica")
    outer_grad = summed / lax.axis_size("replica")
    new_momentum = OUTER_MOMENTUM * momentum + outer_grad
    outer_step = outer_grad + OUTER_MOMENTUM * new_momentum
    same_group = (owner_list[:, None] == owner_list[None, :]).astype(jnp.float32)
    outer_rate = rate_table[layer_kind[:, 0], layer_kind[:, 1]]
    squares = lax.psum(jnp.sum(outer_step * outer_step, axis=(1, 2)), "fsdp")
    group_squares = jnp.sum(same_group * squares[None, :], axis=1)
    group_count = jnp.sum(same_group, axis=1)
    scaling = lax.rsqrt(group_squares / (group_count * (all_rows * rank_dim)) + EPSILON)
    direction = (outer_step * (outer_rate * scaling)[:, None, None]).astype(jnp.bfloat16)
    update = lax.dot_general(
        direction.reshape(-1, rank_dim), projection, (((1,), (1,)), ((), ())),
        preferred_element_type=jnp.float32,
    ).astype(jnp.bfloat16).reshape(anchor_params.shape)
    new_params = (anchor_params.astype(jnp.float32) - update.astype(jnp.float32)).astype(
        jnp.bfloat16
    )
    return (new_params, new_momentum)


def solution(mesh):
    placed = (
        P(None, "fsdp", None),
        P("replica", None, "fsdp", None),
        P(),
        P(None, "fsdp", None),
        P(),
        P(),
        P(),
    )
    return jax.shard_map(
        local,
        mesh=mesh,
        in_specs=placed,
        out_specs=(P(None, "fsdp", None), P(None, "fsdp", None)),
        check_vma=False,
    )
```

profile of v0, /device:TPU:0, one launch (start us, length us, event | category | flops | bytes accessed | tf_op | source)
XLA Modules:
  0.0 138.6 jit_solution(10460643017657377276)
XLA Ops:
  7.2 0.0 copy-start
  7.2 0.0 all-reduce.2.cloned.1.call-start
  7.2 1.8 %copy-done = bf16[4096,384]{1,0:T(8,128)(2,1)S(1)} copy-done((bf16[4096,384]{1,0:T(8,128)(2,1)S(1)}, bf16[4096,384]{1,0:T(8,128)(2,1)}, u32[]{:S(2)}) %copy-start) | copy-done | bytes 3145752
  9.1 13.0 %fusion.2 = f32[24,64,384]{2,1,0:T(8,128)} fusion(bf16[24,64,4096]{2,1,0:T(8,128)(2,1)} %param.7, bf16[1,24,64,4096]{3,2,1,0:T(8,128)(2,1)} %param.8, bf16[4096,384]{1,0:T(8,128)(2,1)S(1)} %copy-done), kind=kOutput, calls=%fused_computation.6 | convolution fusion | flops 4857004032 | bytes 30670848 | tf_op jit(solution)/shard_map/dot_general | solution.py:17
  22.1 0.0 copy-start.3
  22.1 0.0 copy-start.1
  22.1 0.0 all-reduce.2.cloned.1.call-update
  22.1 0.7 copy-done.3
  22.8 0.0 copy-done.1
  22.8 0.8 gather_fusion
  23.6 57.0 %all-reduce.2.cloned.1.call-done = f32[24,64,384]{2,1,0:T(8,128)} async-done(((f32[24,64,384]{2,1,0:T(8,128)}), f32[24,64,384]{2,1,0:T(8,128)}) %all-reduce.2.cloned.1.call-update) | async-done | bytes 2359312 | tf_op jit(solution)/shard_map/psum | solution.py:22
  80.6 4.3 %multiply_reduce_fusion = (f32[24]{0:T(128)S(1)}, f32[24,64,384]{2,1,0:T(8,128)}) fusion(f32[24,64,384]{2,1,0:T(8,128)} %all-reduce.2.cloned.1.call-done, f32[24,64,384]{2,1,0:T(8,128)} %param.10), kind=kLoop, calls=%fused_computation.10 | loop fusion | flops 4128744 | bytes 7077984 | tf_op jit(solution)/shard_map/reduce_sum | solution.py:28
  84.9 21.3 %psum.15 = f32[24]{0:T(128)S(1)} all-reduce(f32[24]{0:T(128)S(1)} %get-tuple-element.4), channel_id=1, replica_groups=mesh['replica'=4,'fsdp'=8] {'fsdp'}, use_global_device_ids=true, to_apply=%region_2.0 | all-reduce | flops 24 | bytes 192 | tf_op jit(solution)/shard_map/psum | solution.py:28
  106.3 0.0 copy-done.2
  106.3 0.2 fusion.7
  106.5 0.0 slice-start
  106.5 3.1 %multiply_convert_fusion = bf16[24,64,384]{2,1,0:T(8,128)(2,1)S(1)} fusion(f32[24]{0:T(128)S(1)} %rsqrt_multiply_fusion, f32[24,64,384]{2,1,0:T(8,128)} %get-tuple-element.5, f32[24,64,384]{2,1,0:T(8,128)} %all-reduce.2.cloned.1.call-done), kind=kLoop, calls=%fused_computation.9 | loop fusion | flops 2949120 | bytes 5898336 | tf_op jit(solution)/shard_map/convert_element_type | solution.py:32
  109.6 0.0 slice-start.1
  109.6 0.0 slice-start.2
  109.6 9.7 %convolution_convert_fusion = bf16[1536,4096]{1,0:T(8,128)(2,1)} fusion(bf16[1536,384]{1,0:T(8,128)(2,1)S(1)} %bitcast.19, bf16[4096,384]{1,0:T(8,128)(2,1)S(1)} %copy-done), kind=kOutput, calls=%fused_computation.5 | convolution fusion | flops 4838129664 | bytes 16908288 | tf_op jit(solution)/shard_map/dot_general | solution.py:33
  119.3 0.0 slice-done
  119.3 0.0 slice-done.1
  119.3 0.0 slice-done.2
  119.3 12.4 %fusion.1 = bf16[24,64,4096]{2,1,0:T(8,128)(2,1)} fusion(bf16[24,64,4096]{2,1,0:T(8,128)(2,1)S(1)} %bitcast.17, bf16[24,64,4096]{2,1,0:T(8,128)(2,1)} %bitcast.18), kind=kLoop, calls=%fused_computation.4 | loop fusion | flops 25165824 | bytes 37748736 | tf_op jit(solution)/shard_map/convert_element_type | solution.py:37
  (4 shorter events, 0.0 us)
Async XLA Ops:
  7.2 1.9 %copy-start = (bf16[4096,384]{1,0:T(8,128)(2,1)S(1)}, bf16[4096,384]{1,0:T(8,128)(2,1)}, u32[]{:S(2)}) copy-start(bf16[4096,384]{1,0:T(8,128)(2,1)} %param.9) | copy-start | bytes 9437188
  7.2 73.4 %all-reduce.2.cloned.1.call-start = ((), (), s32[]{:S(2)}) async-start(), calls=%async_computation | async-start | bytes 4718592 | tf_op jit(solution)/shard_map/psum | solution.py:22
  22.1 0.7 copy-start.3
  22.1 0.7 copy-start.1
  23.6 82.6 %copy-start.2 = (s32[24]{0:T(128)S(1)}, s32[24]{0:T(128)}, u32[]{:S(2)}) copy-start(s32[24]{0:T(128)} %param.12) | copy-start | bytes 292
  106.5 12.8 %slice-start = ((s8[12582912]{0:T(1024)(128)(4,1)}), s8[4194304]{0:T(1024)(128)(4,1)S(1)}, s32[]{:S(2)}) async-start(s8[12582912]{0:T(1024)(128)(4,1)} %bitcast.16), calls=%async_computation.1 | async-start | bytes 8388608
  109.6 9.7 %slice-start.1 = ((s8[12582912]{0:T(1024)(128)(4,1)}), s8[4194304]{0:T(1024)(128)(4,1)S(1)}, s32[]{:S(2)}) async-start(s8[12582912]{0:T(1024)(128)(4,1)} %bitcast.16), calls=%async_computation.2 | async-start | bytes 8388608
  109.6 9.7 %slice-start.2 = ((s8[12582912]{0:T(1024)(128)(4,1)}), s8[4194304]{0:T(1024)(128)(4,1)S(1)}, s32[]{:S(2)}) async-start(s8[12582912]{0:T(1024)(128)(4,1)} %bitcast.16), calls=%async_computation.3 | async-start | bytes 8388608
Sparse Core Ops, SparseCore 0:
  22.2 58.3 all-reduce.1
where the time goes:
time: 139 us
  waiting for transfers between devices  57 us (41%)
  matrix products  22.7 us (16%)
  blocking collectives  21.3 us (15%)
  other arithmetic  20.1 us (14%)
  between operations  14.1 us (10%)
  local copies, waits for them, and re-layouts  3.37 us (2%)
    psum x1, waiting for transfers between devices, local(): lax.psum(compressed.reshape(matrices, rows_dev, rank_dim), 'replica')  57 us
    psum x1, blocking collectives, local(): squares = lax.psum(jnp.sum(outer_step * outer_step, axis=(1, 2)), 'fsdp')  21.3 us
    dot_general x1, matrix products, local(): jnp.dot(pseudo_grad.reshape(matrices * rows_dev, model_width), projection...  13 us
    convert_element_type x1, other arithmetic, local(): (anchor_params.astype(jnp.float32) - update.astype(jnp.float32)).astype(j...  12.4 us
    dot_general x1, matrix products, local(): lax.dot_general(direction.reshape(-1, rank_dim), projection, (((1,), (1,)...  9.7 us
    reduce_sum x1, other arithmetic, local(): squares = lax.psum(jnp.sum(outer_step * outer_step, axis=(1, 2)), 'fsdp')  4.33 us
    convert_element_type x1, other arithmetic, local(): (outer_step * (outer_rate * scaling)[:, None, None]).astype(jnp.bfloat16)  3.09 us
  transfers between devices with their start and end apart: 1, of which 1 were waited for; matrix products, arithmetic and copies ran while one was open for 1% of the time, Pallas kernels for 0%

commit v1 on v0

v1 whole, which is shorter than its diff:
```python
import functools
import jax
import jax.numpy as jnp
from jax import lax
from jax.experimental import pallas as pl
from jax.experimental.pallas import tpu as pltpu
from jax.sharding import PartitionSpec as P

OUTER_MOMENTUM = 0.9
EPSILON = 1e-06
CHUNKS = 6
CORES = 2
F32 = jnp.float32
BF16 = jnp.bfloat16


def reduce_kernel(matrices, n_replica, n_fsdp, *refs):
    (anchor, replica, proj, mom,
     anchor_v, proj_v, step_v, nm_v, sq_v,
     rep_v, mom_v, comp_v, prec_v, ys_v, og_v, sq_all,
     a_sem, r_sem, one_sem, p_send, p_recv, y_send, y_recv, q_send, q_recv, s_send, s_recv) = refs
    rows, width = anchor.shape
    rank = proj.shape[1]
    per = matrices // CHUNKS
    size = rows // CHUNKS
    half = size // CORES
    n_y = n_replica // CORES
    rep = lax.axis_index("replica")
    f = lax.axis_index("fsdp")
    y = rep // CORES
    core = rep % CORES
    partner = y * CORES + 1 - core

    def load(k):
        rs = pl.ds(k * size, size)
        return (pltpu.make_async_copy(anchor.at[rs], anchor_v.at[rs], a_sem.at[k]),
                pltpu.make_async_copy(replica.at[rs], rep_v.at[rs], r_sem.at[k]))

    pcopy = pltpu.make_async_copy(proj, proj_v, one_sem.at[0])
    mcopy = pltpu.make_async_copy(mom, mom_v, one_sem.at[1])
    pcopy.start()
    for k in range(2):
        for c in load(k):
            c.start()

    barrier = pltpu.get_barrier_semaphore()
    pl.semaphore_signal(barrier, inc=1, device_id={"replica": partner})
    for d in range(1, n_y):
        pl.semaphore_signal(barrier, inc=1, device_id={"replica": lax.rem(y + d, n_y) * CORES + core})
    for d in range(1, n_fsdp):
        pl.semaphore_signal(barrier, inc=1, device_id={"fsdp": lax.rem(f + d, n_fsdp)})

    mine = pl.multiple_of(core * half, half)
    theirs = pl.multiple_of((1 - core) * half, half)

    def p_copy(k):
        return pltpu.make_async_remote_copy(
            comp_v.at[k, pl.ds(theirs, half)], prec_v.at[k], p_send.at[k], p_recv.at[k],
            device_id={"replica": partner})

    def y_copy(k, d, slot):
        return pltpu.make_async_remote_copy(
            ys_v.at[slot, k], ys_v.at[slot, k], y_send.at[d - 1, k], y_recv.at[d - 1, k],
            device_id={"replica": lax.rem(y + d, n_y) * CORES + core})

    def q_copy(k, off):
        return pltpu.make_async_remote_copy(
            og_v.at[k, pl.ds(off, half)], og_v.at[k, pl.ds(off, half)], q_send.at[k], q_recv.at[k],
            device_id={"replica": partner})

    def s_copy(d, slot):
        return pltpu.make_async_remote_copy(
            sq_all.at[slot], sq_all.at[slot], s_send.at[d - 1], s_recv.at[d - 1],
            device_id={"fsdp": lax.rem(f + d, n_fsdp)})

    def stage_a(k):
        if k == 0:
            pcopy.wait()
        for c in load(k):
            c.wait()
        if k + 2 < CHUNKS:
            for c in load(k + 2):
                c.start()
        if k + 2 == CHUNKS:
            mcopy.start()
        rs = pl.ds(k * size, size)
        pseudo = (anchor_v[rs, :].astype(F32) - rep_v[rs, :].astype(F32)).astype(BF16)
        comp_v[k] = jnp.dot(pseudo, proj_v[...], preferred_element_type=F32)
        if k == 0:
            pl.semaphore_wait(barrier, 1 + (n_y - 1) + (n_fsdp - 1))
        p_copy(k).start()

    def stage_b(k):
        p_copy(k).wait_recv()
        ys_v[y, k] = (comp_v[k, pl.ds(mine, half)] + prec_v[k]).astype(BF16)
        for d in range(1, n_y):
            y_copy(k, d, y).start()

    def stage_c(k):
        for d in range(1, n_y):
            y_copy(k, d, lax.rem(y + n_y - d, n_y)).wait_recv()
        total = ys_v[0, k].astype(F32)
        for i in range(1, n_y):
            total = total + ys_v[i, k].astype(F32)
        og_v[k, pl.ds(mine, half)] = total * (1.0 / n_replica)
        q_copy(k, mine).start()

    def stage_d(k):
        if k == 0:
            mcopy.wait()
        q_copy(k, theirs).wait_recv()
        rs = pl.ds(k * size, size)
        grad = og_v[k]
        moved = OUTER_MOMENTUM * mom_v[rs, :] + grad
        nm_v[rs, :] = moved
        step = grad + OUTER_MOMENTUM * moved
        step_v[rs, :] = step
        square = jnp.sum((step * step).reshape(per, rows // matrices, rank), axis=1)
        lanes = square[:, :128]
        for i in range(1, rank // 128):
            lanes = lanes + square[:, i * 128:(i + 1) * 128]
        sq_all[f, pl.ds(k * per, per), :] = lanes

    for k in range(CHUNKS + 1):
        if k < CHUNKS:
            stage_a(k)
        if k >= 1:
            stage_b(k - 1)
    for k in range(CHUNKS + 1):
        if k < CHUNKS:
            stage_c(k)
        if k >= 1:
            stage_d(k - 1)
    for d in range(1, n_fsdp):
        s_copy(d, f).start()
    for k in range(CHUNKS):
        p_copy(k).wait_send()
        for d in range(1, n_y):
            y_copy(k, d, y).wait_send()
        q_copy(k, mine).wait_send()
    for d in range(1, n_fsdp):
        s_copy(d, lax.rem(f + n_fsdp - d, n_fsdp)).wait_recv()
    total = sq_all[0]
    for i in range(1, n_fsdp):
        total = total + sq_all[i]
    sq_v[...] = total
    for d in range(1, n_fsdp):
        s_copy(d, f).wait_send()


def apply_kernel(matrices, entries, anchor_v, proj_v, step_v, nm_v, sq_v, rates, owners, kinds,
                 new_params, new_mom, out_v, fac_v, o_sem, m_sem):
    rows, width = anchor_v.shape
    rank = proj_v.shape[1]
    mcopy = pltpu.make_async_copy(nm_v, new_mom, m_sem)
    mcopy.start()
    lane = sq_v.shape[1]
    index = lax.broadcasted_iota(jnp.int32, (matrices, lane), 0)
    owner = jnp.zeros((matrices, lane), jnp.int32)
    rate = jnp.zeros((matrices, lane), F32)
    for m in range(matrices):
        owner = jnp.where(index == m, owners[m], owner)
        rate = jnp.where(index == m, rates[kinds[m, 0], kinds[m, 1]], rate)
    group = jnp.zeros((matrices, lane), F32)
    count = jnp.zeros((matrices, lane), F32)
    for m in range(matrices):
        same = owner == owners[m]
        group = group + jnp.where(same, sq_v[pl.ds(m, 1), :], 0.0)
        count = count + jnp.where(same, 1.0, 0.0)
    group = jnp.sum(group, axis=1, keepdims=True)
    fac_v[...] = rate * lax.rsqrt(group / (count * entries) + EPSILON)
    per = matrices // CHUNKS
    each = rows // matrices
    size = rows // CHUNKS

    def out_copy(k):
        return pltpu.make_async_copy(out_v.at[k % 2], new_params.at[pl.ds(k * size, size)], o_sem.at[k % 2])

    tile = 1024
    for k in range(CHUNKS):
        if k >= 2:
            out_copy(k - 2).wait()
        parts = []
        for i in range(per):
            m = k * per + i
            parts.append(step_v[pl.ds(m * each, each), :] * fac_v[pl.ds(m, 1), 0:1])
        direction = jnp.concatenate(parts, axis=0).astype(BF16)
        for j in range(width // tile):
            cs = pl.ds(j * tile, tile)
            update = lax.dot_general(direction, proj_v[cs, :], (((1,), (1,)), ((), ())),
                                     preferred_element_type=F32).astype(BF16)
            out_v[k % 2, :, cs] = (anchor_v[pl.ds(k * size, size), cs].astype(F32)
                                   - update.astype(F32)).astype(BF16)
        out_copy(k).start()
    for k in range(CHUNKS - 2, CHUNKS):
        out_copy(k).wait()
    mcopy.wait()


def local(anchor_params, replica_params, projection, momentum, rate_table, owner_list, layer_kind):
    matrices, rows_dev, width = anchor_params.shape
    rank = projection.shape[1]
    n_replica = lax.axis_size("replica")
    n_fsdp = lax.axis_size("fsdp")
    n_y = n_replica // CORES
    rows = matrices * rows_dev
    size = rows // CHUNKS
    half = size // CORES
    anchor = anchor_params.reshape(rows, width)
    replica = replica_params.reshape(rows, width)
    any_spec = pl.BlockSpec(memory_space=pl.ANY)
    vmem = pl.BlockSpec(memory_space=pltpu.VMEM)
    smem = pl.BlockSpec(memory_space=pltpu.SMEM)
    dma = pltpu.SemaphoreType.DMA
    held = pl.pallas_call(
        functools.partial(reduce_kernel, matrices, n_replica, n_fsdp),
        out_shape=(
            pltpu.VMEM((rows, width), BF16),
            pltpu.VMEM((width, rank), BF16),
            pltpu.VMEM((rows, rank), F32),
            pltpu.VMEM((rows, rank), F32),
            pltpu.VMEM((matrices, 128), F32),
        ),
        in_specs=[any_spec] * 4,
        out_specs=(vmem,) * 5,
        scratch_shapes=[
            pltpu.VMEM((rows, width), BF16),
            pltpu.VMEM((rows, rank), F32),
            pltpu.VMEM((CHUNKS, size, rank), F32),
            pltpu.VMEM((CHUNKS, half, rank), F32),
            pltpu.VMEM((n_y, CHUNKS, half, rank), BF16),
            pltpu.VMEM((CHUNKS, size, rank), F32),
            pltpu.VMEM((n_fsdp, matrices, 128), F32),
            dma((CHUNKS,)), dma((CHUNKS,)), dma((2,)),
            dma((CHUNKS,)), dma((CHUNKS,)),
            dma((n_y - 1, CHUNKS)), dma((n_y - 1, CHUNKS)),
            dma((CHUNKS,)), dma((CHUNKS,)),
            dma((n_fsdp - 1,)), dma((n_fsdp - 1,)),
        ],
        compiler_params=pltpu.CompilerParams(
            collective_id=0, has_side_effects=True, vmem_limit_bytes=32 * 1024 * 1024),
    )(anchor, replica, projection, momentum.reshape(rows, rank))
    new_params, new_mom = pl.pallas_call(
        functools.partial(apply_kernel, matrices, float(rows_dev * n_fsdp * rank)),
        out_shape=(
            jax.ShapeDtypeStruct((rows, width), BF16),
            jax.ShapeDtypeStruct((rows, rank), F32),
        ),
        in_specs=[vmem] * 5 + [smem] * 3,
        out_specs=(any_spec, any_spec),
        scratch_shapes=[
            pltpu.VMEM((2, size, width), BF16),
            pltpu.VMEM((matrices, 128), F32),
            dma((2,)), dma(()),
        ],
        compiler_params=pltpu.CompilerParams(vmem_limit_bytes=24 * 1024 * 1024),
    )(*held, rate_table, owner_list, layer_kind)
    return new_params.reshape(anchor_params.shape), new_mom.reshape(momentum.shape)


def solution(mesh):
    placed = (
        P(None, "fsdp", None),
        P("replica", None, "fsdp", None),
        P(),
        P(None, "fsdp", None),
        P(),
        P(),
        P(),
    )
    return jax.shard_map(
        local,
        mesh=mesh,
        in_specs=placed,
        out_specs=(P(None, "fsdp", None), P(None, "fsdp", None)),
        check_vma=False,
    )
```

time: 139 us -> 53.3 us (0.38)
  waiting for transfers between devices: 57 us -> 0 us
  Pallas kernels: 0 us -> 40.5 us
  matrix products: 22.7 us -> 0 us
  blocking collectives: 21.3 us -> 0 us
  other arithmetic: 20.1 us -> 0 us
  between operations: 14.1 us -> 0.81 us
  local copies, waits for them, and re-layouts: 3.37 us -> 11.8 us
    psum x1 -> x0, waiting for transfers between devices: 57 us -> none  [local(): lax.psum(compressed.reshape(matrices, rows_dev, rank_dim), 'replica')]
    pallas_call x0 -> x2, Pallas kernels: none -> 40.5 us  [the longest x1 30 us: local(): pl.pallas_call(functools.partial(reduce_kernel, matrices, n_replica, n_fs...]
    dot_general x2 -> x0, matrix products: 22.7 us -> none  [the longest x1 13 us: local(): jnp.dot(pseudo_grad.reshape(matrices * rows_dev, model_width), projection...]
    psum x1 -> x0, blocking collectives: 21.3 us -> none  [local(): squares = lax.psum(jnp.sum(outer_step * outer_step, axis=(1, 2)), 'fsdp')]
    convert_element_type x2 -> x0, other arithmetic: 15.5 us -> none  [the longest x1 12.4 us: local(): (anchor_params.astype(jnp.float32) - update.astype(jnp.float32)).astype(j...]
    unnamed x14 -> x11, local copies, waits for them, and re-layouts: 2.52 us -> 11.8 us
    reduce_sum x2 -> x0, other arithmetic: 4.51 us -> none  [the longest x1 4.33 us: local(): squares = lax.psum(jnp.sum(outer_step * outer_step, axis=(1, 2)), 'fsdp')]
  transfers between devices with their start and end apart: 1 -> 0, of which waited for: 1 -> 0; matrix products, arithmetic and copies ran while one was open for 1% -> 0% of each run, Pallas kernels for 0% -> 0%
where the time goes in v1:
time: 53.3 us; the launch traced here: 53.1 us
  Pallas kernels  40.5 us (76%)
  local copies, waits for them, and re-layouts  11.8 us (22%)
  between operations  0.81 us (2%)
    pallas_call x1, Pallas kernels, local(): pl.pallas_call(functools.partial(reduce_kernel, matrices, n_replica, n_fs...  30 us
    unnamed x11, local copies, waits for them, and re-layouts  11.8 us
    pallas_call x1, Pallas kernels, local(): pl.pallas_call(functools.partial(apply_kernel, matrices, float(rows_dev *...  10.5 us

profile of v1, /device:TPU:0, one launch (start us, length us, event | category | flops | bytes accessed | tf_op | source)
XLA Modules:
  0.0 53.1 jit_solution(11124284730262255584)
XLA Ops:
  0.6 0.8 %copy.9.kinds = s32[24,2]{1,0:T(8,128)S(1)} copy(s32[24,2]{0,1:T(2,128)} %param.13) | data formatting | bytes 384 | tf_op args[6]
  1.4 0.0 copy-start.2
  1.4 1.7 %copy-done.2 = f32[24,64,384]{2,1,0:T(8,128)S(1)} copy-done((f32[24,64,384]{2,1,0:T(8,128)S(1)}, f32[24,64,384]{2,1,0:T(8,128)}, u32[]{:S(2)}) %copy-start.2) | copy-done | bytes 2359320
  3.1 0.0 copy-start.3
  3.1 0.0 copy-start.4
  3.1 30.0 %shard_map.86 = (bf16[1536,4096]{1,0:T(8,128)(2,1)S(1)}, bf16[4096,384]{1,0:T(8,128)(2,1)S(1)}, f32[1536,384]{1,0:T(8,128)S(1)}, f32[1536,384]{1,0:T(8,128)S(1)}, f32[24,128]{1,0:T(8,128)S(1)}) custom-call(bf16[1536,4096]{1,0:T(8,128)(2,1)} %bitcast.6, bf16[1536,4096]{1,0:T(8,128)(2,1)} %bitcast.7, bf16[4096,384]{1,0:T(8,128)(2,1)} %refs_2_.1, ...), custom_call_target="tpu_custom_call" | custom-call | tf_op jit(solution)/shard_map/pallas_call | solution.py:215
  33.0 0.0 copy-start
  33.0 4.8 %copy-done = bf16[1536,4096]{1,0:T(8,128)(2,1)} copy-done((bf16[1536,4096]{1,0:T(8,128)(2,1)}, bf16[1536,4096]{1,0:T(8,128)(2,1)S(1)}, u32[]{:S(2)}) %copy-start) | copy-done | bytes 12582936
  37.8 0.0 copy-done.3
  37.8 0.0 copy-done.4
  37.8 0.0 copy-start.1
  37.8 4.6 %copy-done.1 = bf16[1536,4096]{1,0:T(8,128)(2,1)S(1)} copy-done((bf16[1536,4096]{1,0:T(8,128)(2,1)S(1)}, bf16[1536,4096]{1,0:T(8,128)(2,1)}, u32[]{:S(2)}) %copy-start.1) | copy-done | bytes 12582936
  42.4 10.5 %shard_map.87 = (bf16[1536,4096]{1,0:T(8,128)(2,1)}, f32[1536,384]{1,0:T(8,128)}) custom-call(bf16[1536,4096]{1,0:T(8,128)(2,1)S(1)} %copy-done.1, bf16[4096,384]{1,0:T(8,128)(2,1)S(1)} %get-tuple-element.10.proj_v, f32[1536,384]{1,0:T(8,128)S(1)} %get-tuple-element.11.step_v, f32[1536,384]{1,0:T(8,128)S(1)} %get-tuple-element.12.nm_v, ...), custom_call_target="tpu_custom_call" | custom-call | tf_op jit(solution)/shard_map/pallas_call | solution.py:243
Async XLA Ops:
  1.4 1.7 %copy-start.2 = (f32[24,64,384]{2,1,0:T(8,128)S(1)}, f32[24,64,384]{2,1,0:T(8,128)}, u32[]{:S(2)}) copy-start(f32[24,64,384]{2,1,0:T(8,128)} %param.10) | copy-start | bytes 7077892
  3.1 34.8 %copy-start.3 = (f32[4,6]{1,0:T(4,128)S(1)}, f32[4,6]{1,0:T(4,128)}, u32[]{:S(2)}) copy-start(f32[4,6]{1,0:T(4,128)} %rates.1) | copy-start | bytes 292
  3.1 34.8 %copy-start.4 = (s32[24]{0:T(128)S(1)}, s32[24]{0:T(128)}, u32[]{:S(2)}) copy-start(s32[24]{0:T(128)} %owners.1) | copy-start | bytes 292
  33.0 4.8 %copy-start = (bf16[1536,4096]{1,0:T(8,128)(2,1)}, bf16[1536,4096]{1,0:T(8,128)(2,1)S(1)}, u32[]{:S(2)}) copy-start(bf16[1536,4096]{1,0:T(8,128)(2,1)S(1)} %get-tuple-element.9.anchor_v) | copy-start | bytes 37748740
  37.8 4.6 %copy-start.1 = (bf16[1536,4096]{1,0:T(8,128)(2,1)S(1)}, bf16[1536,4096]{1,0:T(8,128)(2,1)}, u32[]{:S(2)}) copy-start(bf16[1536,4096]{1,0:T(8,128)(2,1)} %copy-done) | copy-start | bytes 37748740
